TPU v7x, 32 devices: a whole 2x2x4 slice. The times are simulated.
32 devices in a mesh: section: 4 (over z), expert: 4 (over y, x), dp: 2 (over core).
Axes of the slice: x: 2, y: 2, z: 4, core: 2. Of those that a mesh axis runs over, the one named last changes fastest.
Arguments:
- tokens_fwd: bfloat16 [2048, 2560], P(('section', 'expert', 'dp')), may hold values from -6 to 6
- route_fwd: int32 [2048], P(('section', 'expert', 'dp')), may hold values from 0 to 1, as said below
- gate_fwd: float32 [2048], P(('section', 'expert', 'dp')), may hold values from 0.2 to 1
- grad_out: bfloat16 [2048, 2560], P(('section', 'expert', 'dp')), may hold values from -3 to 3
- route_bwd: int32 [2048], P(('section', 'expert', 'dp')), may hold values from 0 to 1, as said below
- gate_bwd: float32 [2048], P(('section', 'expert', 'dp')), may hold values from 0.2 to 1
- saved_pre: bfloat16 [4, 2, 128, 1536], P('section', 'dp', None, 'expert'), may hold values from -6 to 6
- w_up: bfloat16 [4, 2560, 1536], P('section', None, 'expert'), may hold values from -0.125 to 0.125
- w_down: bfloat16 [4, 1536, 2560], P('section', 'expert'), may hold values from -0.21875 to 0.21875
- basis_q: float32 [2560, 64], replicated, may hold values from -6 to 6
Outputs:
- expert_out: bfloat16 [2048, 2560], P(('section', 'expert', 'dp'))
- grad_in: bfloat16 [2048, 2560], P(('section', 'expert', 'dp'))
- factor_p: float32 [4, 1536, 64], P('section', 'expert')
- factor_q: bfloat16 [4, 4, 2560, 64], P('section', 'expert')
Inputs may be any that keep to these rules, and one draw needn't show every extreme that they name: `route_fwd`: each device's 64 tokens name each of the 2 live experts exactly 32 times. `route_bwd`: each device's 64 tokens name each of the 2 live experts exactly 32 times.
All inputs are finite; a program needn't handle non-finite values.
Results may differ from a plain program's by a relative error of at most 0.0065.
Values may be sent and summed in bfloat16 or wider, within the bound.
A program may use at most 64 MiB of HBM per device.

v0:
```python
import functools

import jax
import jax.numpy as jnp
from jax import lax
from jax.experimental import pallas as pl
from jax.experimental.pallas import tpu as pltpu
from jax.sharding import PartitionSpec as P

highest = lax.Precision.HIGHEST
MESH = pl.DeviceIdType.MESH


def from_partner(value, axis, apart):
    mask = 2**apart
    pairs = [(source, source ^ mask) for source in range(lax.axis_size(axis))]
    return lax.ppermute(value, axis, pairs)


def orthonormal(matrix):
    column_count = matrix.shape[1]

    def place_column(position, result):
        column = lax.dynamic_slice_in_dim(matrix, position, 1, 1)
        earlier = (jnp.arange(column_count, dtype=jnp.int32) < position).astype(matrix.dtype)[
            :, None
        ]
        for repeat in range(2):
            project = jnp.dot(result.T, column, precision=highest) * earlier
            column = column - jnp.dot(result, project, precision=highest)
        column = column * lax.rsqrt(jnp.sum(column * column) + 1e-06)
        return lax.dynamic_update_slice_in_dim(result, column, position, 1)

    return lax.fori_loop(0, column_count, place_column, jnp.zeros_like(matrix))


def contract_last(left, right):
    return lax.dot_general(
        left, right, (((1,), (1,)), ((), ())), preferred_element_type=jnp.float32
    )


def spread_rows(picked):
    device_count = lax.axis_size("expert")
    experts_live = picked.shape[0]
    capacity = picked.shape[1]
    features = picked.shape[2]
    return jnp.broadcast_to(picked[:, None], (experts_live, 2, capacity, features)).reshape(
        device_count, capacity, features
    )


def send_rows(first_picked, second_picked):
    first_out = spread_rows(first_picked)
    second_out = spread_rows(second_picked)
    first_arrived, second_arrived = [
        lax.all_to_all(element, "expert", split_axis=0, concat_axis=0, tiled=True)
        for element in (first_out, second_out)
    ]
    features = first_arrived.shape[2]
    return (first_arrived.reshape(-1, features), second_arrived.reshape(-1, features))


def collect_rows(returned, experts_live):
    features = returned.shape[2]
    capacity = returned.shape[1]
    summed = returned.reshape(experts_live, 2, capacity, features).astype(jnp.float32)
    return (summed[:, 0] + summed[:, 1]).astype(jnp.bfloat16).reshape(-1, features)


def send_back(first_partial, second_partial, experts_live):
    device_count = lax.axis_size("expert")
    features = first_partial.shape[1]
    capacity = first_partial.shape[0] // device_count
    first_out = first_partial.reshape(device_count, capacity, features).astype(jnp.bfloat16)
    second_out = second_partial.reshape(device_count, capacity, features).astype(jnp.bfloat16)
    first_returned, second_returned = [
        lax.all_to_all(element, "expert", split_axis=0, concat_axis=0, tiled=True)
        for element in (first_out, second_out)
    ]
    return (collect_rows(first_returned, experts_live), collect_rows(second_returned, experts_live))


def pair_total(local_term):
    mirrored = local_term
    for bit_level in range(lax.axis_size("section").bit_length() - 1):
        mirrored = from_partner(mirrored, "section", bit_level)
    return lax.psum(local_term + mirrored, "dp")


def body(
    tokens_fwd, route_fwd, gate_fwd, grad_out, route_bwd, gate_bwd, saved_pre, w_up, w_down, basis_q
):
    device_count = lax.axis_size("expert")
    experts_live = device_count // 2
    token_count = tokens_fwd.shape[0]
    features = tokens_fwd.shape[1]
    capacity = token_count // experts_live
    up_cols = w_up[0]
    down_rows = w_down[0]
    order_fwd = jnp.argsort(route_fwd, stable=True)
    inverse_fwd = jnp.argsort(order_fwd)
    scaled = (gate_bwd[:, None] * grad_out.astype(jnp.float32)).astype(jnp.bfloat16)
    order_bwd = jnp.argsort(route_bwd, stable=True)
    inverse_bwd = jnp.argsort(order_bwd)
    inputs, grad_rows = send_rows(
        tokens_fwd[order_fwd].reshape(experts_live, capacity, features),
        scaled[order_bwd].reshape(experts_live, capacity, features),
    )
    hidden = jax.nn.silu(jnp.dot(inputs, up_cols, preferred_element_type=jnp.float32)).astype(
        jnp.bfloat16
    )
    partial_value = jnp.dot(hidden, down_rows, preferred_element_type=jnp.float32)
    preact = saved_pre[0, 0].astype(jnp.float32)
    sigmoid_pre = jax.nn.sigmoid(preact)
    hidden_bwd = (preact * sigmoid_pre).astype(jnp.bfloat16)
    slope_term = sigmoid_pre * (1.0 + preact * (1.0 - sigmoid_pre))
    pre_grad = (contract_last(grad_rows, down_rows) * slope_term).astype(jnp.bfloat16)
    input_part = contract_last(pre_grad, up_cols)
    mixed_sorted, grad_sorted = send_back(partial_value, input_part, experts_live)
    expert_out = (gate_fwd[:, None] * mixed_sorted[inverse_fwd].astype(jnp.float32)).astype(
        jnp.bfloat16
    )
    grad_in = grad_sorted[inverse_bwd]
    weight_grad = lax.dot_general(
        hidden_bwd, grad_rows, (((0,), (0,)), ((), ())), preferred_element_type=jnp.float32
    )
    left_term = jnp.dot(weight_grad, basis_q, precision=highest)
    left_factor = orthonormal(pair_total(left_term))
    right_term = lax.dot_general(
        weight_grad,
        left_factor,
        (((0,), (0,)), ((), ())),
        precision=highest,
        preferred_element_type=jnp.float32,
    )
    right_factor = pair_total(right_term).astype(jnp.bfloat16)
    return (expert_out, grad_in, left_factor[None], right_factor[None, None])


def slot_matrix(route_row, capacity):
    count = route_row.shape[1]
    first = lax.broadcasted_iota(jnp.int32, (count, count), 0)
    second = lax.broadcasted_iota(jnp.int32, (count, count), 1)
    across = jnp.broadcast_to(route_row.astype(jnp.float32), (count, count))
    down = jnp.sum(jnp.where(first == second, across, 0.0), axis=1, keepdims=True)
    ahead = jnp.where((down == across) & (first < second), 1.0, 0.0)
    slot = across * capacity + jnp.sum(ahead, axis=0, keepdims=True)
    return jnp.where(slot == first.astype(jnp.float32), 1.0, 0.0).astype(jnp.bfloat16)


def as_column(row):
    count = row.shape[1]
    first = lax.broadcasted_iota(jnp.int32, (count, count), 0)
    second = lax.broadcasted_iota(jnp.int32, (count, count), 1)
    return jnp.sum(jnp.where(first == second, row, 0.0), axis=1, keepdims=True)


def halves(value):
    high = value.astype(jnp.bfloat16)
    return high, (value - high.astype(jnp.float32)).astype(jnp.bfloat16)


def dot32(left, right, dims=((1,), (0,))):
    return lax.dot_general(left, right, (dims, ((), ())), preferred_element_type=jnp.float32)


def fused_kernel(
    sizes,
    tok_hbm, rf_ref, gf_ref, go_hbm, rb_ref, gb_ref, pre_hbm, up_hbm, down_hbm, basis_hbm,
    out_ref, gin_ref, p_ref, q_ref,
    tok_ref, go_ref, pre_ref, up, down, basis, sendz, sendx, zbuf, xbuf, partb, partf, retb, retf,
    lown, lpeer, lsum, lpart, amat, umat, rown, rpeer, rsum, zout, zin, qbuf,
    local_sem, zs, zr, xs, xr, bs, br, fs, fr, ps, pr,
):
    n, n_sec, cap = sizes
    live = n // 2
    me = lax.axis_index("expert")
    core = lax.axis_index("dp")
    sibling = {"dp": 1 - core}
    mirror = {"section": n_sec - 1 - lax.axis_index("section")}

    loads = [
        pltpu.make_async_copy(source, target, local_sem.at[i])
        for i, (source, target) in enumerate(
            (
                (go_hbm, go_ref), (tok_hbm, tok_ref), (pre_hbm, pre_ref),
                (basis_hbm, basis), (down_hbm, down), (up_hbm, up),
            )
        )
    ]
    for load in loads:
        load.start()

    barrier = pltpu.get_barrier_semaphore()
    for shift in range(1, n):
        pl.semaphore_signal(
            barrier, inc=1, device_id={"expert": lax.rem(me + shift, n)}, device_id_type=MESH
        )
    pl.semaphore_signal(barrier, inc=1, device_id=sibling, device_id_type=MESH)
    pl.semaphore_signal(barrier, inc=1, device_id=mirror, device_id_type=MESH)

    def rows_of(index):
        return pl.ds(pl.multiple_of(index * cap, cap), cap)

    def remote(source, target, send, recv, device):
        return pltpu.make_async_remote_copy(
            src_ref=source, dst_ref=target, send_sem=send, recv_sem=recv,
            device_id=device, device_id_type=MESH,
        )

    def dispatch(source, target, send, recv):
        copies = []
        for shift in range(1, n):
            to = lax.rem(me + shift, n)
            copies.append(
                remote(source.at[rows_of(to // 2)], target.at[rows_of(me)],
                       send.at[shift], recv.at[shift], {"expert": to})
            )
        for copy in copies:
            copy.start()
        target[rows_of(me)] = source[rows_of(me // 2)]
        return copies

    def send_back(source, target, send, recv):
        copies = []
        for shift in range(1, n):
            to = lax.rem(me + shift, n)
            copies.append(
                remote(source.at[rows_of(to)], target.at[rows_of(me)],
                       send.at[shift], recv.at[shift], {"expert": to})
            )
        for copy in copies:
            copy.start()
        target[rows_of(me)] = source[rows_of(me)]
        return copies

    def combine(returned):
        sums = [
            (
                returned[2 * e * cap : (2 * e + 1) * cap].astype(jnp.float32)
                + returned[(2 * e + 1) * cap : (2 * e + 2) * cap].astype(jnp.float32)
            ).astype(jnp.bfloat16)
            for e in range(live)
        ]
        return jnp.concatenate(sums, axis=0)

    place_bwd = slot_matrix(rb_ref[...], cap)
    loads[0].wait()
    scaled = (as_column(gb_ref[...]) * go_ref[...].astype(jnp.float32)).astype(jnp.bfloat16)
    sendz[...] = dot32(place_bwd, scaled).astype(jnp.bfloat16)
    pl.semaphore_wait(barrier, n + 1)
    z_copies = dispatch(sendz, zbuf, zs, zr)
    place_fwd = slot_matrix(rf_ref[...], cap)
    loads[1].wait()
    sendx[...] = dot32(place_fwd, tok_ref[...]).astype(jnp.bfloat16)
    x_copies = dispatch(sendx, xbuf, xs, xr)

    loads[2].wait()
    preact = pre_ref[...].astype(jnp.float32)
    sigmoid = jax.nn.sigmoid(preact)
    hidden_bwd = (preact * sigmoid).astype(jnp.bfloat16)
    slope = sigmoid * (1.0 + preact * (1.0 - sigmoid))

    loads[3].wait()
    basis_high, basis_low = halves(basis[...])
    for copy in z_copies:
        copy.wait()
    nt = ((1,), (1,))
    zb_high, zb_low = halves(dot32(basis_high, zbuf[...], nt) + dot32(basis_low, zbuf[...], nt))
    lown[...] = dot32(zb_high, hidden_bwd) + dot32(zb_low, hidden_bwd)
    left_dp = remote(lown, lpeer, ps.at[0], pr.at[0], sibling)
    left_dp.start()

    loads[4].wait()
    pre_grad = (dot32(zbuf[...], down[...], ((1,), (1,))) * slope).astype(jnp.bfloat16)
    left_dp.wait()
    lsum[...] = lown[...] + lpeer[...]
    left_z = remote(lsum, lpart, ps.at[1], pr.at[1], mirror)
    left_z.start()
    loads[5].wait()
    partb[...] = dot32(pre_grad, up[...], ((1,), (1,))).astype(jnp.bfloat16)
    b_copies = send_back(partb, retb, bs, br)

    for copy in x_copies:
        copy.wait()
    value = dot32(xbuf[...], up[...])
    hidden = (value * jax.nn.sigmoid(value)).astype(jnp.bfloat16)
    partf[...] = dot32(hidden, down[...]).astype(jnp.bfloat16)
    f_copies = send_back(partf, retf, fs, fr)

    left_z.wait()
    amat[...] = lsum[...] + lpart[...]
    umat[...] = jnp.zeros_like(umat)
    rank = amat.shape[0]

    def place(k, v):
        earlier = umat[...]
        follow = amat[pl.ds(lax.rem(k + 1, rank), 1), :]
        again = jnp.sum(earlier * v, axis=1, keepdims=True)
        ahead = jnp.sum(earlier * follow, axis=1, keepdims=True)
        v = v - jnp.sum(earlier * again, axis=0, keepdims=True)
        follow_left = follow - jnp.sum(earlier * ahead, axis=0, keepdims=True)
        square = jnp.sum(v * v, axis=1, keepdims=True)
        share = jnp.sum(v * follow, axis=1, keepdims=True)
        inverse = lax.rsqrt(square + 1e-06)
        unit = v * inverse
        umat[pl.ds(k, 1), :] = unit
        return follow_left - unit * (share * inverse)

    lax.fori_loop(0, rank, place, amat[pl.ds(0, 1), :])
    p_ref[...] = umat[...]

    u_high, u_low = halves(umat[...])
    hp_high, hp_low = halves(dot32(u_high, hidden_bwd, nt) + dot32(u_low, hidden_bwd, nt))
    rown[...] = dot32(hp_high, zbuf[...]) + dot32(hp_low, zbuf[...])
    half = rank // 2
    mine = pl.ds(pl.multiple_of(core * half, half), half)
    other = pl.ds(pl.multiple_of((1 - core) * half, half), half)
    right_dp = remote(rown.at[other], rpeer, ps.at[2], pr.at[2], sibling)
    right_dp.start()
    for copy in b_copies:
        copy.wait()
    gin_ref[...] = dot32(place_bwd, combine(retb), ((0,), (0,))).astype(jnp.bfloat16)
    right_dp.wait()
    rsum[...] = rown[mine] + rpeer[...]
    zout[...] = rsum[...].astype(jnp.bfloat16)
    right_z = remote(zout, zin, ps.at[3], pr.at[3], mirror)
    right_z.start()
    for copy in f_copies:
        copy.wait()
    mixed = dot32(place_fwd, combine(retf), ((0,), (0,)))
    out_ref[...] = (as_column(gf_ref[...]) * mixed).astype(jnp.bfloat16)
    right_z.wait()
    qbuf[mine] = (rsum[...] + zin[...].astype(jnp.float32)).astype(jnp.bfloat16)
    share_q = remote(qbuf.at[mine], qbuf.at[mine], ps.at[4], pr.at[4], sibling)
    share_q.start()
    share_q.wait()
    q_ref[...] = qbuf[...]


def fused_body(
    tokens_fwd, route_fwd, gate_fwd, grad_out, route_bwd, gate_bwd, saved_pre, w_up, w_down, basis_q
):
    n, n_sec = lax.axis_size("expert"), lax.axis_size("section")
    count, features = tokens_fwd.shape
    cap = count // (n // 2)
    slots, units = saved_pre.shape[2:]
    rank = basis_q.shape[1]
    bf, f32 = jnp.bfloat16, jnp.float32
    vmem = pl.BlockSpec(memory_space=pltpu.VMEM)
    hbm = pl.BlockSpec(memory_space=pl.ANY)
    wide = [pltpu.VMEM((slots, features), bf)]
    square = [pltpu.VMEM((rank, units), f32)]
    half = (rank // 2, features)
    expert_out, grad_in, left, right = pl.pallas_call(
        functools.partial(fused_kernel, (n, n_sec, cap)),
        out_shape=(
            jax.ShapeDtypeStruct((count, features), bf),
            jax.ShapeDtypeStruct((count, features), bf),
            jax.ShapeDtypeStruct((rank, units), f32),
            jax.ShapeDtypeStruct((rank, features), bf),
        ),
        in_specs=[hbm, vmem, vmem, hbm, vmem, vmem, hbm, hbm, hbm, hbm],
        out_specs=(vmem,) * 4,
        scratch_shapes=[
            pltpu.VMEM((count, features), bf),
            pltpu.VMEM((count, features), bf),
            pltpu.VMEM((slots, units), bf),
            pltpu.VMEM((features, units), bf),
            pltpu.VMEM((units, features), bf),
            pltpu.VMEM((rank, features), f32),
            pltpu.VMEM((count, features), bf),
            pltpu.VMEM((count, features), bf),
        ]
        + wide * 4
        + [pltpu.VMEM((n * cap, features), bf)] * 2
        + square * 6
        + [
            pltpu.VMEM((rank, features), f32),
            pltpu.VMEM(half, f32),
            pltpu.VMEM(half, f32),
            pltpu.VMEM(half, bf),
            pltpu.VMEM(half, bf),
            pltpu.VMEM((rank, features), bf),
            pltpu.SemaphoreType.DMA((6,)),
        ]
        + [pltpu.SemaphoreType.DMA((n,))] * 8
        + [pltpu.SemaphoreType.DMA((5,))] * 2,
        compiler_params=pltpu.CompilerParams(
            collective_id=0, has_side_effects=True, vmem_limit_bytes=63 * 2**20
        ),
    )(
        tokens_fwd, route_fwd[None], gate_fwd[None], grad_out, route_bwd[None], gate_bwd[None],
        saved_pre[0, 0], w_up[0], w_down[0], basis_q.T,
    )
    return (expert_out, grad_in, left.T[None], right.T[None, None])


def solution(mesh):
    def choose(*arguments):
        n = lax.axis_size("expert")
        capacity = arguments[0].shape[0] // (n // 2)
        rank = arguments[9].shape[1]
        whole_tiles = capacity % 16 == 0 and rank % 32 == 0
        pairs = lax.axis_size("dp") == 2 and lax.axis_size("section") % 2 == 0
        return (fused_body if whole_tiles and pairs else body)(*arguments)

    return jax.shard_map(
        choose,
        mesh=mesh,
        in_specs=(
            P(("section", "expert", "dp"), None),
            P(("section", "expert", "dp")),
            P(("section", "expert", "dp")),
            P(("section", "expert", "dp"), None),
            P(("section", "expert", "dp")),
            P(("section", "expert", "dp")),
            P("section", "dp", None, "expert"),
            P("section", None, "expert"),
            P("section", "expert", None),
            P(),
        ),
        out_specs=(
            P(("section", "expert", "dp"), None),
            P(("section", "expert", "dp"), None),
            P("section", "expert", None),
            P("section", "expert", None, None),
        ),
        check_vma=False,
    )
```

profile of v0, /device:TPU:0, one launch (start us, length us, event | category | flops | bytes accessed | tf_op | source)
XLA Modules:
  0.0 54.9 jit_solution(13158847699280717861)
XLA Ops:
  0.6 47.6 %shard_map.129 = (bf16[64,2560]{1,0:T(8,128)(2,1)}, bf16[64,2560]{1,0:T(8,128)(2,1)}, f32[64,384]{1,0:T(8,128)}, bf16[64,2560]{1,0:T(8,128)(2,1)}) custom-call(bf16[64,2560]{1,0:T(8,128)(2,1)} %tok_hbm.1, s32[1,64]{1,0:T(1,128)} %bitcast.20, f32[1,64]{1,0:T(1,128)} %bitcast.21, bf16[64,2560]{1,0:T(8,128)(2,1)} %go_hbm.1, s32[1,64]{1,0:T(1,128)} %bitcast.22, ...), custom_call_target="tpu_custom_call" | custom-call | tf_op jit(solution)/shard_map/pallas_call | solution.py:356
  48.2 1.7 %copy.18 = bf16[64,2560]{1,0:T(8,128)(2,1)} copy(bf16[64,2560]{1,0:T(8,128)(2,1)} %get-tuple-element.16) | data formatting | bytes 655360
  50.0 1.7 %copy.19 = bf16[64,2560]{1,0:T(8,128)(2,1)} copy(bf16[64,2560]{1,0:T(8,128)(2,1)} %get-tuple-element.17) | data formatting | bytes 655360
  51.7 1.5 %copy.20 = f32[1,384,64]{1,2,0:T(8,128)} copy(f32[1,384,64]{1,2,0:T(8,128)} %bitcast.18) | data formatting | bytes 196608
  53.2 1.7 %copy.21 = bf16[1,1,2560,64]{2,3,1,0:T(8,128)(2,1)} copy(bf16[1,1,2560,64]{2,3,1,0:T(8,128)(2,1)} %bitcast.17) | data formatting | bytes 655360
where the time goes:
time: 55.9 us; the launch traced here: 54.9 us
  Pallas kernels  47.6 us (85%)
  local copies, waits for them, and re-layouts  6.69 us (12%)
  between operations  0.64 us (1%)
    pallas_call x1, Pallas kernels, fused_body(): pl.pallas_call(functools.partial(fused_kernel, (n, n_sec, cap)), out_shap...  47.6 us
    unnamed x4, local copies, waits for them, and re-layouts  6.69 us

commit v1 on v0

--- a/solution.py
+++ b/solution.py
@@ -9,6 +9,8 @@
 
 highest = lax.Precision.HIGHEST
 MESH = pl.DeviceIdType.MESH
+BLOCK = 16
+VMEM_LIMIT = 63 * 2**20
 
 
 def from_partner(value, axis, apart):
@@ -171,7 +173,8 @@
     out_ref, gin_ref, p_ref, q_ref,
     tok_ref, go_ref, pre_ref, up, down, basis, sendz, sendx, zbuf, xbuf, partb, partf, retb, retf,
     lown, lpeer, lsum, lpart, amat, umat, rown, rpeer, rsum, zout, zin, qbuf,
-    local_sem, zs, zr, xs, xr, bs, br, fs, fr, ps, pr,
+    hb_ref, slope_ref, terms, terms_in,
+    local_sem, zs, zr, xs, xr, bs, br, fs, fr, ts, tr, ps, pr,
 ):
     n, n_sec, cap = sizes
     live = n // 2
@@ -184,8 +187,8 @@
         pltpu.make_async_copy(source, target, local_sem.at[i])
         for i, (source, target) in enumerate(
             (
-                (go_hbm, go_ref), (tok_hbm, tok_ref), (pre_hbm, pre_ref),
-                (basis_hbm, basis), (down_hbm, down), (up_hbm, up),
+                (go_hbm, go_ref), (basis_hbm, basis), (tok_hbm, tok_ref),
+                (pre_hbm, pre_ref), (down_hbm, down), (up_hbm, up),
             )
         )
     ]
@@ -249,53 +252,45 @@
     loads[0].wait()
     scaled = (as_column(gb_ref[...]) * go_ref[...].astype(jnp.float32)).astype(jnp.bfloat16)
     sendz[...] = dot32(place_bwd, scaled).astype(jnp.bfloat16)
+    loads[1].wait()
+    basis_high, basis_low = halves(basis[...])
+    nt = ((1,), (1,))
+    terms[...] = dot32(sendz[...], basis_high, nt) + dot32(sendz[...], basis_low, nt)
     pl.semaphore_wait(barrier, n + 1)
+    t_copies = dispatch(terms, terms_in, ts, tr)
     z_copies = dispatch(sendz, zbuf, zs, zr)
     place_fwd = slot_matrix(rf_ref[...], cap)
-    loads[1].wait()
+    loads[2].wait()
     sendx[...] = dot32(place_fwd, tok_ref[...]).astype(jnp.bfloat16)
     x_copies = dispatch(sendx, xbuf, xs, xr)
 
-    loads[2].wait()
+    loads[3].wait()
     preact = pre_ref[...].astype(jnp.float32)
     sigmoid = jax.nn.sigmoid(preact)
-    hidden_bwd = (preact * sigmoid).astype(jnp.bfloat16)
-    slope = sigmoid * (1.0 + preact * (1.0 - sigmoid))
-
-    loads[3].wait()
-    basis_high, basis_low = halves(basis[...])
-    for copy in z_copies:
+    hb_ref[...] = (preact * sigmoid).astype(jnp.bfloat16)
+
+    for copy in t_copies:
         copy.wait()
-    nt = ((1,), (1,))
-    zb_high, zb_low = halves(dot32(basis_high, zbuf[...], nt) + dot32(basis_low, zbuf[...], nt))
-    lown[...] = dot32(zb_high, hidden_bwd) + dot32(zb_low, hidden_bwd)
+    zb_high, zb_low = halves(terms_in[...].T)
+    lown[...] = dot32(zb_high, hb_ref[...]) + dot32(zb_low, hb_ref[...])
     left_dp = remote(lown, lpeer, ps.at[0], pr.at[0], sibling)
     left_dp.start()
-
-    loads[4].wait()
-    pre_grad = (dot32(zbuf[...], down[...], ((1,), (1,))) * slope).astype(jnp.bfloat16)
+    slope_ref[...] = sigmoid * (1.0 + preact * (1.0 - sigmoid))
+    umat[...] = jnp.zeros_like(umat)
     left_dp.wait()
     lsum[...] = lown[...] + lpeer[...]
     left_z = remote(lsum, lpart, ps.at[1], pr.at[1], mirror)
     left_z.start()
-    loads[5].wait()
-    partb[...] = dot32(pre_grad, up[...], ((1,), (1,))).astype(jnp.bfloat16)
-    b_copies = send_back(partb, retb, bs, br)
-
-    for copy in x_copies:
-        copy.wait()
-    value = dot32(xbuf[...], up[...])
-    hidden = (value * jax.nn.sigmoid(value)).astype(jnp.bfloat16)
-    partf[...] = dot32(hidden, down[...]).astype(jnp.bfloat16)
-    f_copies = send_back(partf, retf, fs, fr)
-
     left_z.wait()
     amat[...] = lsum[...] + lpart[...]
-    umat[...] = jnp.zeros_like(umat)
     rank = amat.shape[0]
-
-    def place(k, v):
-        earlier = umat[...]
+    features = rown.shape[1]
+    span = features // 2
+    mine = pl.ds(pl.multiple_of(core * span, 128), span)
+    other = pl.ds(pl.multiple_of((1 - core) * span, 128), span)
+
+    def place(reach, k, v):
+        earlier = umat[0:reach]
         follow = amat[pl.ds(lax.rem(k + 1, rank), 1), :]
         again = jnp.sum(earlier * v, axis=1, keepdims=True)
         ahead = jnp.sum(earlier * follow, axis=1, keepdims=True)
@@ -308,35 +303,102 @@
         umat[pl.ds(k, 1), :] = unit
         return follow_left - unit * (share * inverse)
 
-    lax.fori_loop(0, rank, place, amat[pl.ds(0, 1), :])
-    p_ref[...] = umat[...]
-
-    u_high, u_low = halves(umat[...])
-    hp_high, hp_low = halves(dot32(u_high, hidden_bwd, nt) + dot32(u_low, hidden_bwd, nt))
-    rown[...] = dot32(hp_high, zbuf[...]) + dot32(hp_low, zbuf[...])
-    half = rank // 2
-    mine = pl.ds(pl.multiple_of(core * half, half), half)
-    other = pl.ds(pl.multiple_of((1 - core) * half, half), half)
-    right_dp = remote(rown.at[other], rpeer, ps.at[2], pr.at[2], sibling)
-    right_dp.start()
+    def columns(block):
+        return slice(block * BLOCK, (block + 1) * BLOCK)
+
+    def both(high, low):
+        return jnp.concatenate([high, low], axis=0)
+
+    def right_copies(block):
+        rows, first = pl.ds(block * BLOCK, BLOCK), 2 + 3 * block
+        return (
+            remote(rown.at[rows, other], rpeer.at[rows], ps.at[first], pr.at[first], sibling),
+            remote(zout.at[rows], zin.at[rows], ps.at[first + 1], pr.at[first + 1], mirror),
+            remote(qbuf.at[rows, mine], qbuf.at[rows, mine],
+                   ps.at[first + 2], pr.at[first + 2], sibling),
+        )
+
+    def right_begin(block):
+        hp = dot32(both(*halves(umat[columns(block)])), hb_ref[...], nt)
+        right = dot32(both(*halves(hp[:BLOCK] + hp[BLOCK:])), zbuf[...])
+        rown[columns(block)] = right[:BLOCK] + right[BLOCK:]
+        rights[block][0].start()
+
+    def right_mirror(block):
+        rights[block][0].wait()
+        rsum[columns(block)] = rown[columns(block), mine] + rpeer[columns(block)]
+        zout[columns(block)] = rsum[columns(block)].astype(jnp.bfloat16)
+        rights[block][1].start()
+
+    def right_share(block):
+        rights[block][1].wait()
+        total = rsum[columns(block)] + zin[columns(block)].astype(jnp.float32)
+        qbuf[columns(block), mine] = total.astype(jnp.bfloat16)
+        rights[block][2].start()
+
+    blocks = rank // BLOCK
+    rights = [right_copies(block) for block in range(blocks)]
+    v = amat[pl.ds(0, 1), :]
+    for block in range(blocks):
+        middle, top = block * BLOCK + BLOCK // 2, (block + 1) * BLOCK
+        v = lax.fori_loop(block * BLOCK, middle, functools.partial(place, middle), v)
+        if block >= 1:
+            right_mirror(block - 1)
+        v = lax.fori_loop(middle, top, functools.partial(place, top), v)
+        if block == 0:
+            for copy in z_copies:
+                copy.wait()
+        right_begin(block)
+        if block >= 1:
+            right_share(block - 1)
+        if block == 0:
+            loads[4].wait()
+            pre_grad = dot32(zbuf[...], down[...], nt) * slope_ref[...]
+            loads[5].wait()
+            partb[...] = dot32(pre_grad.astype(jnp.bfloat16), up[...], nt).astype(jnp.bfloat16)
+            b_copies = send_back(partb, retb, bs, br)
+        if block == min(1, blocks - 1):
+            for copy in x_copies:
+                copy.wait()
+            value = dot32(xbuf[...], up[...])
+            hidden = (value * jax.nn.sigmoid(value)).astype(jnp.bfloat16)
+            partf[...] = dot32(hidden, down[...]).astype(jnp.bfloat16)
+            f_copies = send_back(partf, retf, fs, fr)
     for copy in b_copies:
         copy.wait()
     gin_ref[...] = dot32(place_bwd, combine(retb), ((0,), (0,))).astype(jnp.bfloat16)
-    right_dp.wait()
-    rsum[...] = rown[mine] + rpeer[...]
-    zout[...] = rsum[...].astype(jnp.bfloat16)
-    right_z = remote(zout, zin, ps.at[3], pr.at[3], mirror)
-    right_z.start()
+    right_mirror(blocks - 1)
+    p_ref[...] = umat[...]
     for copy in f_copies:
         copy.wait()
     mixed = dot32(place_fwd, combine(retf), ((0,), (0,)))
     out_ref[...] = (as_column(gf_ref[...]) * mixed).astype(jnp.bfloat16)
-    right_z.wait()
-    qbuf[mine] = (rsum[...] + zin[...].astype(jnp.float32)).astype(jnp.bfloat16)
-    share_q = remote(qbuf.at[mine], qbuf.at[mine], ps.at[4], pr.at[4], sibling)
-    share_q.start()
-    share_q.wait()
+    right_share(blocks - 1)
+    for copies in rights:
+        copies[2].wait()
     q_ref[...] = qbuf[...]
+
+
+def finish_kernel(*refs):
+    count = len(refs) // 2
+    copies = [
+        pltpu.make_async_copy(refs[i], refs[count + i], refs[-1].at[i]) for i in range(count)
+    ]
+    for copy in copies:
+        copy.start()
+    for copy in copies:
+        copy.wait()
+
+
+def finish(arrays):
+    return pl.pallas_call(
+        finish_kernel,
+        out_shape=tuple(jax.ShapeDtypeStruct(a.shape, a.dtype) for a in arrays),
+        in_specs=[pl.BlockSpec(memory_space=pl.ANY)] * len(arrays),
+        out_specs=(pl.BlockSpec(memory_space=pltpu.VMEM),) * len(arrays),
+        scratch_shapes=[pltpu.SemaphoreType.DMA((len(arrays),))],
+        compiler_params=pltpu.CompilerParams(vmem_limit_bytes=VMEM_LIMIT),
+    )(*arrays)
 
 
 def fused_body(
@@ -349,11 +411,11 @@
     rank = basis_q.shape[1]
     bf, f32 = jnp.bfloat16, jnp.float32
     vmem = pl.BlockSpec(memory_space=pltpu.VMEM)
-    hbm = pl.BlockSpec(memory_space=pl.ANY)
+    hbm = pl.BlockSpec(memory_space=pltpu.HBM)
     wide = [pltpu.VMEM((slots, features), bf)]
     square = [pltpu.VMEM((rank, units), f32)]
-    half = (rank // 2, features)
-    expert_out, grad_in, left, right = pl.pallas_call(
+    half = (rank, features // 2)
+    results = pl.pallas_call(
         functools.partial(fused_kernel, (n, n_sec, cap)),
         out_shape=(
             jax.ShapeDtypeStruct((count, features), bf),
@@ -383,17 +445,22 @@
             pltpu.VMEM(half, bf),
             pltpu.VMEM(half, bf),
             pltpu.VMEM((rank, features), bf),
+            pltpu.VMEM((slots, units), bf),
+            pltpu.VMEM((slots, units), f32),
+            pltpu.VMEM((count, rank), f32),
+            pltpu.VMEM((slots, rank), f32),
             pltpu.SemaphoreType.DMA((6,)),
         ]
-        + [pltpu.SemaphoreType.DMA((n,))] * 8
-        + [pltpu.SemaphoreType.DMA((5,))] * 2,
+        + [pltpu.SemaphoreType.DMA((n,))] * 10
+        + [pltpu.SemaphoreType.DMA((2 + 3 * (rank // BLOCK),))] * 2,
         compiler_params=pltpu.CompilerParams(
-            collective_id=0, has_side_effects=True, vmem_limit_bytes=63 * 2**20
+            collective_id=0, has_side_effects=True, vmem_limit_bytes=VMEM_LIMIT
         ),
     )(
         tokens_fwd, route_fwd[None], gate_fwd[None], grad_out, route_bwd[None], gate_bwd[None],
         saved_pre[0, 0], w_up[0], w_down[0], basis_q.T,
     )
+    expert_out, grad_in, left, right = finish(results)
     return (expert_out, grad_in, left.T[None], right.T[None, None])
 
 
@@ -402,7 +469,8 @@
         n = lax.axis_size("expert")
         capacity = arguments[0].shape[0] // (n // 2)
         rank = arguments[9].shape[1]
-        whole_tiles = capacity % 16 == 0 and rank % 32 == 0
+        whole_tiles = capacity % 16 == 0 and rank % BLOCK == 0
+        whole_tiles = whole_tiles and arguments[0].shape[1] % 256 == 0
         pairs = lax.axis_size("dp") == 2 and lax.axis_size("section") % 2 == 0
         return (fused_body if whole_tiles and pairs else body)(*arguments)
 

time: 55.9 us -> 49.4 us (0.88); the launches traced: 54.9 us -> 49.1 us
  local copies, waits for them, and re-layouts: 6.69 us -> 0 us
  Pallas kernels: 47.6 us -> 48.5 us
    unnamed x4 -> x0, local copies, waits for them, and re-layouts: 6.69 us -> none
    pallas_call x0 -> x1, Pallas kernels: none -> 2.21 us  [finish(): pl.pallas_call(finish_kernel, out_shape=tuple((jax.ShapeDtypeStruct(a.sha...]
    pallas_call x1, Pallas kernels: 47.6 us -> 46.3 us  [fused_body(): pl.pallas_call(functools.partial(fused_kernel, (n, n_sec, cap)), out_shap...]
where the time goes in v1:
time: 49.4 us; the launch traced here: 49.1 us
  Pallas kernels  48.5 us (98%)
  between operations  0.64 us (1%)
    pallas_call x1, Pallas kernels, fused_body(): pl.pallas_call(functools.partial(fused_kernel, (n, n_sec, cap)), out_shap...  46.3 us
    pallas_call x1, Pallas kernels, finish(): pl.pallas_call(finish_kernel, out_shape=tuple((jax.ShapeDtypeStruct(a.sha...  2.21 us

profile of v1, /device:TPU:0, one launch (start us, length us, event | category | flops | bytes accessed | tf_op | source)
XLA Modules:
  0.0 49.1 jit_solution(3655560611397992623)
XLA Ops:
  0.6 46.3 %shard_map.129 = (bf16[64,2560]{1,0:T(8,128)(2,1)}, bf16[64,2560]{1,0:T(8,128)(2,1)}, f32[64,384]{1,0:T(8,128)}, bf16[64,2560]{1,0:T(8,128)(2,1)}) custom-call(bf16[64,2560]{1,0:T(8,128)(2,1)} %tok_hbm.1, s32[1,64]{1,0:T(1,128)} %bitcast.18, f32[1,64]{1,0:T(1,128)} %bitcast.19, bf16[64,2560]{1,0:T(8,128)(2,1)} %go_hbm.1, s32[1,64]{1,0:T(1,128)} %bitcast.20, ...), custom_call_target="tpu_custom_call" | custom-call | tf_op jit(solution)/shard_map/pallas_call | solution.py:418
  46.9 2.2 %shard_map.130 = (bf16[64,2560]{1,0:T(8,128)(2,1)}, bf16[64,2560]{1,0:T(8,128)(2,1)}, f32[64,384]{1,0:T(8,128)}, bf16[64,2560]{1,0:T(8,128)(2,1)}) custom-call(bf16[64,2560]{1,0:T(8,128)(2,1)} %get-tuple-element.12.refs_0_, bf16[64,2560]{1,0:T(8,128)(2,1)} %get-tuple-element.13.refs_1_, f32[64,384]{1,0:T(8,128)} %get-tuple-element.14.refs_2_, ...), custom_call_target="tpu_custom_call" | custom-call | tf_op jit(solution)/shard_map/pallas_call | solution.py:394

commit v2 on v1

--- a/solution.py
+++ b/solution.py
@@ -279,11 +279,21 @@
     umat[...] = jnp.zeros_like(umat)
     left_dp.wait()
     lsum[...] = lown[...] + lpeer[...]
-    left_z = remote(lsum, lpart, ps.at[1], pr.at[1], mirror)
-    left_z.start()
-    left_z.wait()
-    amat[...] = lsum[...] + lpart[...]
     rank = amat.shape[0]
+    blocks = rank // BLOCK
+    lefts = [
+        remote(lsum.at[pl.ds(block * BLOCK, BLOCK)], lpart.at[pl.ds(block * BLOCK, BLOCK)],
+               ps.at[1 + block], pr.at[1 + block], mirror)
+        for block in range(blocks)
+    ]
+    for copy in lefts:
+        copy.start()
+
+    def left_arrives(block):
+        lefts[block].wait()
+        rows = slice(block * BLOCK, (block + 1) * BLOCK)
+        amat[rows] = lsum[rows] + lpart[rows]
+
     features = rown.shape[1]
     span = features // 2
     mine = pl.ds(pl.multiple_of(core * span, 128), span)
@@ -310,7 +320,7 @@
         return jnp.concatenate([high, low], axis=0)
 
     def right_copies(block):
-        rows, first = pl.ds(block * BLOCK, BLOCK), 2 + 3 * block
+        rows, first = pl.ds(block * BLOCK, BLOCK), 1 + blocks + 3 * block
         return (
             remote(rown.at[rows, other], rpeer.at[rows], ps.at[first], pr.at[first], sibling),
             remote(zout.at[rows], zin.at[rows], ps.at[first + 1], pr.at[first + 1], mirror),
@@ -336,21 +346,23 @@
         qbuf[columns(block), mine] = total.astype(jnp.bfloat16)
         rights[block][2].start()
 
-    blocks = rank // BLOCK
     rights = [right_copies(block) for block in range(blocks)]
+    left_arrives(0)
     v = amat[pl.ds(0, 1), :]
     for block in range(blocks):
         middle, top = block * BLOCK + BLOCK // 2, (block + 1) * BLOCK
         v = lax.fori_loop(block * BLOCK, middle, functools.partial(place, middle), v)
         if block >= 1:
             right_mirror(block - 1)
+        if block >= 2:
+            right_share(block - 2)
+        if block + 1 < blocks:
+            left_arrives(block + 1)
         v = lax.fori_loop(middle, top, functools.partial(place, top), v)
         if block == 0:
             for copy in z_copies:
                 copy.wait()
         right_begin(block)
-        if block >= 1:
-            right_share(block - 1)
         if block == 0:
             loads[4].wait()
             pre_grad = dot32(zbuf[...], down[...], nt) * slope_ref[...]
@@ -373,6 +385,8 @@
         copy.wait()
     mixed = dot32(place_fwd, combine(retf), ((0,), (0,)))
     out_ref[...] = (as_column(gf_ref[...]) * mixed).astype(jnp.bfloat16)
+    if blocks >= 2:
+        right_share(blocks - 2)
     right_share(blocks - 1)
     for copies in rights:
         copies[2].wait()
@@ -452,7 +466,7 @@
             pltpu.SemaphoreType.DMA((6,)),
         ]
         + [pltpu.SemaphoreType.DMA((n,))] * 10
-        + [pltpu.SemaphoreType.DMA((2 + 3 * (rank // BLOCK),))] * 2,
+        + [pltpu.SemaphoreType.DMA((1 + 4 * (rank // BLOCK),))] * 2,
         compiler_params=pltpu.CompilerParams(
             collective_id=0, has_side_effects=True, vmem_limit_bytes=VMEM_LIMIT
         ),

time: 49.4 us -> 44.2 us (0.89)
  Pallas kernels: 48.5 us -> 43.3 us
    pallas_call x1, Pallas kernels: 46.3 us -> 41.1 us  [fused_body(): pl.pallas_call(functools.partial(fused_kernel, (n, n_sec, cap)), out_shap...]
where the time goes in v2:
time: 44.2 us; the launch traced here: 44 us
  Pallas kernels  43.3 us (98%)
  between operations  0.64 us (1%)
    pallas_call x1, Pallas kernels, fused_body(): pl.pallas_call(functools.partial(fused_kernel, (n, n_sec, cap)), out_shap...  41.1 us
    pallas_call x1, Pallas kernels, finish(): pl.pallas_call(finish_kernel, out_shape=tuple((jax.ShapeDtypeStruct(a.sha...  2.21 us

profile of v2, /device:TPU:0, one launch (start us, length us, event | category | flops | bytes accessed | tf_op | source)
XLA Modules:
  0.0 44.0 jit_solution(13575494242006871530)
XLA Ops:
  0.6 41.1 %shard_map.129 = (bf16[64,2560]{1,0:T(8,128)(2,1)}, bf16[64,2560]{1,0:T(8,128)(2,1)}, f32[64,384]{1,0:T(8,128)}, bf16[64,2560]{1,0:T(8,128)(2,1)}) custom-call(bf16[64,2560]{1,0:T(8,128)(2,1)} %tok_hbm.1, s32[1,64]{1,0:T(1,128)} %bitcast.18, f32[1,64]{1,0:T(1,128)} %bitcast.19, bf16[64,2560]{1,0:T(8,128)(2,1)} %go_hbm.1, s32[1,64]{1,0:T(1,128)} %bitcast.20, ...), custom_call_target="tpu_custom_call" | custom-call | tf_op jit(solution)/shard_map/pallas_call | solution.py:432
  41.8 2.2 %shard_map.130 = (bf16[64,2560]{1,0:T(8,128)(2,1)}, bf16[64,2560]{1,0:T(8,128)(2,1)}, f32[64,384]{1,0:T(8,128)}, bf16[64,2560]{1,0:T(8,128)(2,1)}) custom-call(bf16[64,2560]{1,0:T(8,128)(2,1)} %get-tuple-element.12.refs_0_, bf16[64,2560]{1,0:T(8,128)(2,1)} %get-tuple-element.13.refs_1_, f32[64,384]{1,0:T(8,128)} %get-tuple-element.14.refs_2_, ...), custom_call_target="tpu_custom_call" | custom-call | tf_op jit(solution)/shard_map/pallas_call | solution.py:408
